TPU v7x, 256 devices: a whole 4x4x8 slice. The times are simulated.
256 devices in a mesh: frame: 8 (over z), row: 32 (over x, y, core).
Axes of the slice: x: 4, y: 4, z: 8, core: 2. Of those that a mesh axis runs over, the one named last changes fastest.
Arguments:
- inputs: bfloat16 [64, 128, 128, 256], P('frame', 'row'), may hold values from -6 to 6
- temporal_weight: bfloat16 [3, 256, 256], replicated, may hold values from -0.21875 to 0.21875
- spatial_weight: bfloat16 [3, 3, 256, 256], replicated, may hold values from -0.125 to 0.125
- pooled_grad: bfloat16 [32, 128, 128, 256], P('frame', 'row'), may hold values from -6 to 6
Outputs:
- input_grad: bfloat16 [64, 128, 128, 256], P('frame', 'row')
- temporal_grad: float32 [3, 256, 256], replicated
- spatial_grad: float32 [3, 3, 256, 256], replicated
All inputs are finite; a program needn't handle non-finite values.
Results may differ from a plain program's by a relative error of at most 0.0049.
Values may be sent and summed in bfloat16 or wider, within the bound.
A program may use at most 64 MiB of HBM per device.

v0:
```python
import functools

import jax
import jax.numpy as jnp
from jax import lax
from jax.experimental import pallas as pl
from jax.experimental.pallas import tpu as pltpu
from jax.sharding import PartitionSpec as P

MESH = pl.DeviceIdType.MESH
F32 = jnp.float32
BF16 = jnp.bfloat16
PIPES = 4
BLOCK = 768


def dot(left, right):
    return jnp.dot(left, right, preferred_element_type=F32)


def dot_t(left, right):
    return lax.dot_general(left, right, (((1,), (1,)), ((), ())), preferred_element_type=F32)


def kernel(nz, n, scale, x_hbm, tw_hbm, sw_hbm, g_hbm, outs, tgrad, sgrad,
           xin, gp, tw, sw, u, gacc, gext, ft3, gt, taps, part,
           sb0, rb0, sb1, rb1, own1, zb, ag, other,
           local_sem, halo_send, halo_recv, send_sem, recv_sem, relay):
    nframes, nrows, ncols, chans = x_hbm.shape
    npairs = nframes // 2
    pix = nrows * ncols
    z = lax.axis_index("frame")
    row = lax.axis_index("row")
    nrow = 2 * n * n
    core = row % 2
    y = (row // 2) % n
    x = row // (2 * n)
    chip = row // 2
    mate = (z, row + 1 - 2 * core)

    def plane_index(o):
        return (x + o // n) % n * n + (y + o % n) % n

    def peer_xy(o):
        return (z, 2 * plane_index(o) + core)

    def peer_z(o):
        return ((z + o) % nz, row)

    plane = sorted(range(1, n * n), key=lambda o: -min(o // n, n - o // n) - min(o % n, n - o % n))
    ring = sorted(range(1, nz), key=lambda o: -min(o, nz - o))
    down, up = (z, (row + 1) % nrow), (z, (row + nrow - 1) % nrow)
    nxt, prv = peer_z(1), peer_z(nz - 1)

    loads = [
        pltpu.make_async_copy(g_hbm, gp.at[:, pl.ds(1, nrows)], local_sem.at[0]),
        pltpu.make_async_copy(sw_hbm, sw, local_sem.at[1]),
        pltpu.make_async_copy(tw_hbm, tw, local_sem.at[2]),
        pltpu.make_async_copy(x_hbm, xin.at[pl.ds(1, nframes)], local_sem.at[3]),
    ]
    barrier = pltpu.get_barrier_semaphore()
    outer = (z, (row + nrow + 2 * core - 1) % nrow)
    around = [peer_xy(1), peer_xy(n - 1), peer_xy(n), peer_xy(n * (n - 1)), nxt, prv]
    for device in [mate, outer] + around:
        pl.semaphore_signal(barrier, inc=1, device_id=device, device_id_type=MESH)
    for load in loads:
        load.start()
    pl.semaphore_wait(barrier, 2 + len(around))

    def pass_on(k):
        for device in around:
            pl.semaphore_signal(relay.at[k], inc=1, device_id=device, device_id_type=MESH)

    def hear(k):
        pl.semaphore_wait(relay.at[k], len(around))

    def remote(src, dst, sends, recvs, slot, device):
        return pltpu.make_async_remote_copy(
            src_ref=src, dst_ref=dst, send_sem=sends.at[slot], recv_sem=recvs.at[slot],
            device_id=device, device_id_type=MESH)

    def halo(src, dst, slot, device):
        return remote(src, dst, halo_send, halo_recv, slot, device)

    x_next = halo(x_hbm.at[nframes - 1], xin.at[0], 2, nxt)
    x_prev = halo(x_hbm.at[0], xin.at[nframes + 1], 3, prv)
    rows_down = halo(g_hbm.at[:, nrows - 1], gp.at[:, 0], 0, down)
    rows_up = halo(g_hbm.at[:, 0], gp.at[:, nrows + 1], 1, up)
    for copy in (x_next, x_prev, rows_down, rows_up):
        copy.start()

    def frame(i):
        return xin[i].reshape(pix, chans)

    lane = lax.broadcasted_iota(jnp.int32, (chans, pix), 1) % ncols

    def pair_sum(j):
        u[j] = (frame(j).astype(F32) + frame(j + 1).astype(F32)).astype(BF16)

    def features(i):
        total = dot(u[2 * i], tw[0]) + dot(u[2 * i + 1], tw[1]) + dot(u[2 * i + 2], tw[2])
        total = total + (frame(2 * i + 1).astype(F32) + frame(2 * i + 2).astype(F32))
        flip = total.T
        at = pl.ds(i * pix, pix)
        ft3[pl.ds(chans, chans), at] = flip.astype(BF16)
        right = jnp.where(lane == 0, 0.0, pltpu.roll(flip, 1, 1))
        ft3[pl.ds(0, chans), at] = right.astype(BF16)
        left = jnp.where(lane == ncols - 1, 0.0, pltpu.roll(flip, pix - 1, 1))
        ft3[pl.ds(2 * chans, chans), at] = left.astype(BF16)

    def g_rows(i, first, count):
        return gp[i, pl.ds(first, count)].reshape(count * ncols, chans)

    def shifted(wide):
        column = lax.broadcasted_iota(jnp.int32, (wide.shape[0], chans), 0) % ncols
        low, mid, high = (wide[:, b * chans:(b + 1) * chans] for b in range(3))
        low = jnp.where(column == ncols - 1, 0.0, pltpu.roll(low, wide.shape[0] - 1, 0))
        high = jnp.where(column == 0, 0.0, pltpu.roll(high, 1, 0))
        return low + mid + high

    edge = pix - ncols

    def grad_own(i):
        gacc[i] = shifted(dot_t(g_rows(i, 1, nrows), sw[1]))
        gacc[i, pl.ds(0, edge)] += shifted(dot_t(g_rows(i, 2, nrows - 1), sw[0]))
        gacc[i, pl.ds(ncols, edge)] += shifted(dot_t(g_rows(i, 1, nrows - 1), sw[2]))

    def grad_halo():
        first = shifted(dot_t(gp[:, 0].reshape(npairs * ncols, chans), sw[2]))
        final = shifted(dot_t(gp[:, nrows + 1].reshape(npairs * ncols, chans), sw[0]))
        for i in range(npairs):
            gacc[i, pl.ds(0, ncols)] += first[i * ncols:(i + 1) * ncols]
            gacc[i, pl.ds(edge, ncols)] += final[i * ncols:(i + 1) * ncols]

    def grad_done(i):
        grad = 0.5 * gacc[i]
        gext[i + 1] = grad.astype(BF16)
        gt[:, pl.ds(i * pix, pix)] = grad.T.astype(BF16)

    def outer_sum(i, left, first, count):
        return dot(ft3[:, pl.ds(i * pix + left * ncols, count * ncols)], g_rows(i, first, count))

    def spatial_own(a):
        left, first, count = ((0, 2, nrows - 1), (0, 1, nrows), (1, 1, nrows - 1))[a]
        total = outer_sum(1, left, first, count)
        for i in range(2, npairs - 1):
            total = total + outer_sum(i, left, first, count)
        taps[pl.ds(a * BLOCK, BLOCK)] = total

    def spatial_rest(a):
        total = taps[pl.ds(a * BLOCK, BLOCK)]
        for i in range(1, npairs - 1):
            if a == 0:
                total = total + outer_sum(i, nrows - 1, nrows + 1, 1)
            if a == 2:
                total = total + outer_sum(i, 0, 0, 1)
        for i in (0, npairs - 1):
            total = total + outer_sum(i, 0, 2 - a, nrows)
        taps[pl.ds(a * BLOCK, BLOCK)] = total

    def temporal():
        for k in range(3):
            total = dot(gt[:, pl.ds(0, pix)], u[k])
            for i in range(1, npairs):
                total = total + dot(gt[:, pl.ds(i * pix, pix)], u[2 * i + k])
            taps[pl.ds(3 * BLOCK + k * chans, chans)] = total.T

    half = chans // 2
    size = BLOCK // (n * n)
    own_cols = pl.ds(pl.multiple_of(core * half, half), half)
    mate_cols = pl.ds(pl.multiple_of((1 - core) * half, half), half)
    base_z = n * n
    base_g = base_z + nz - 1
    last = base_g + n * n - 1

    def chunk(index):
        return pl.ds(pl.multiple_of(index * size, size), size)

    def link(p, src, dst, slot, device):
        return remote(src, dst, send_sem.at[p], recv_sem.at[p], slot, device)

    def core_copy(p):
        return link(p, sb0.at[p], rb0.at[p], 0, mate)

    def plane_copies(p):
        return [link(p, sb1.at[p, chunk(plane_index(o))], rb1.at[p, o - 1], o, peer_xy(o)) for o in plane]

    def ring_copies(p):
        return [link(p, zb.at[p, z], zb.at[p, z], base_z + o - 1, peer_z(o)) for o in ring]

    def gather_copies(p):
        own = ag.at[p, chunk(chip)]
        return [link(p, own, own, base_g + o - 1, peer_xy(o)) for o in plane]

    def mate_copy(p):
        return link(p, ag.at[p], other.at[p], last, mate)

    def begin(p):
        sb0[p] = taps[pl.ds(p * BLOCK, BLOCK), mate_cols].astype(BF16)
        core_copy(p).start()

    def step_core(p):
        core_copy(p).wait()
        total = taps[pl.ds(p * BLOCK, BLOCK), own_cols] + rb0[p].astype(F32)
        sb1[p] = total.astype(BF16)
        for copy in plane_copies(p):
            copy.start()
        mine = pl.ds(pl.multiple_of(p * BLOCK + chip * size, size), size)
        own1[p] = taps[mine, own_cols] + rb0[p, chunk(chip)].astype(F32)

    def step_plane(p):
        for copy in plane_copies(p):
            copy.wait()
        total = own1[p]
        for o in plane:
            total = total + rb1[p, o - 1].astype(F32)
        zb[p, z] = total.astype(BF16)
        for copy in ring_copies(p):
            copy.start()

    def step_ring(p):
        for copy in ring_copies(p):
            copy.wait()
        total = zb[p, 0].astype(F32)
        for k in range(1, nz):
            total = total + zb[p, k].astype(F32)
        ag[p, chunk(chip)] = total.astype(BF16)
        for copy in gather_copies(p):
            copy.start()

    def finish(p, half_ref, cols):
        value = half_ref[p].astype(F32)
        if p < 3:
            sgrad[pl.ds(p * BLOCK, BLOCK), cols] = value * (0.5 * scale)
        else:
            tgrad[:, cols] = value * scale

    def step_gather(p):
        for copy in gather_copies(p):
            copy.wait()
        mate_copy(p).start()
        finish(p, ag, own_cols)

    def step_mate(p):
        mate_copy(p).wait()
        finish(p, other, mate_cols)

    def put(t, value):
        outs[t] = value.astype(BF16).reshape(nrows, ncols, chans)

    def input_grad(i):
        grad = gext[i + 1]
        base = grad.astype(F32) + dot_t(grad, tw[1])
        first = dot_t(grad, tw[0])
        final = dot_t(grad, tw[2])
        if i == 0:
            part[0] = base + first
        else:
            put(2 * i, base + first + part[2])
            put(2 * i - 1, part[1] + first)
        part[1] = base + final
        part[2] = final

    pass_on(0)
    loads[2].wait()
    loads[3].wait()
    for j in range(1, nframes):
        pair_sum(j)
    hear(0)
    pass_on(1)
    for i in range(1, npairs - 1):
        features(i)
    loads[0].wait()
    loads[1].wait()
    grad_own(0)
    hear(1)
    pass_on(2)
    for i in range(1, npairs):
        grad_own(i)
    for a in range(3):
        spatial_own(a)
    hear(2)

    rows_down.wait()
    rows_up.wait()

    @pl.when(row == 0)
    def _():
        gp[:, 0] = jnp.zeros((npairs, ncols, chans), BF16)

    @pl.when(row == nrow - 1)
    def _():
        gp[:, nrows + 1] = jnp.zeros((npairs, ncols, chans), BF16)

    grad_halo()
    grad_done(0)
    grad_done(npairs - 1)
    grad_prev = halo(gext.at[1], gext.at[npairs + 1], 4, prv)
    grad_next = halo(gext.at[npairs], gext.at[0], 5, nxt)
    grad_prev.start()
    grad_next.start()
    x_next.wait()
    x_prev.wait()

    @pl.when(z == 0)
    def _():
        xin[0] = jnp.zeros((nrows, ncols, chans), BF16)

    @pl.when(z == nz - 1)
    def _():
        xin[nframes + 1] = jnp.zeros((nrows, ncols, chans), BF16)

    pair_sum(0)
    pair_sum(nframes)
    features(0)
    features(npairs - 1)
    spatial_rest(0)
    begin(0)
    spatial_rest(1)
    begin(1)
    step_core(0)
    spatial_rest(2)
    begin(2)
    step_core(1)
    for i in range(1, npairs - 1):
        grad_done(i)
    step_core(2)
    temporal()
    begin(3)
    input_grad(0)
    step_core(3)
    step_plane(0)
    input_grad(1)
    step_plane(1)
    input_grad(2)
    step_plane(2)
    input_grad(3)
    step_plane(3)
    step_ring(0)
    step_ring(1)
    step_ring(2)
    step_ring(3)

    grad_prev.wait()
    grad_next.wait()

    @pl.when(z == 0)
    def _():
        gext[0] = jnp.zeros((pix, chans), BF16)

    @pl.when(z == nz - 1)
    def _():
        gext[npairs + 1] = jnp.zeros((pix, chans), BF16)

    put(0, part[0] + dot_t(gext[0], tw[2]))
    put(nframes - 1, part[1] + dot_t(gext[npairs + 1], tw[0]))
    for p in range(PIPES):
        step_gather(p)
        if p:
            step_mate(p - 1)
    step_mate(PIPES - 1)


def write_out(grad, temporal, spatial, grad_hbm, temporal_hbm, spatial_hbm, sems):
    copies = [pltpu.make_async_copy(grad.at[t], grad_hbm.at[t], sems.at[t]) for t in range(grad.shape[0])]
    held, kept = (temporal, spatial), (temporal_hbm, spatial_hbm)
    for part in range(2):
        for k in range(held[part].shape[0]):
            copies.append(pltpu.make_async_copy(held[part].at[k], kept[part].at[k], sems.at[len(copies)]))
    for copy in copies:
        copy.start()
    for copy in copies:
        copy.wait()


def solution(mesh):
    nz = mesh.shape["frame"]
    n = 1
    while 2 * n * n < mesh.shape["row"]:
        n += 1

    def body(inputs, temporal_weight, spatial_weight, pooled_grad):
        nframes, nrows, ncols, chans = inputs.shape
        npairs = nframes // 2
        pix = nrows * ncols
        half = chans // 2
        size = BLOCK // (n * n)
        scale = float(nframes * nz * nrows * mesh.shape["row"] * ncols) ** -0.5
        slots = 2 * n * n + nz - 1
        any_spec = pl.BlockSpec(memory_space=pltpu.HBM)
        vmem_spec = pl.BlockSpec(memory_space=pltpu.VMEM)
        spatial = spatial_weight.reshape(3, 3 * chans, chans)
        input_grad, temporal_grad, spatial_grad = pl.pallas_call(
            functools.partial(kernel, nz, n, scale),
            out_shape=[
                pltpu.VMEM(inputs.shape, BF16),
                pltpu.VMEM((3 * chans, chans), F32),
                pltpu.VMEM((9 * chans, chans), F32),
            ],
            in_specs=[any_spec] * 4,
            out_specs=[vmem_spec] * 3,
            scratch_shapes=[
                pltpu.VMEM((nframes + 2, nrows, ncols, chans), BF16),
                pltpu.VMEM((npairs, nrows + 2, ncols, chans), BF16),
                pltpu.VMEM((3, chans, chans), BF16),
                pltpu.VMEM((3, 3 * chans, chans), BF16),
                pltpu.VMEM((nframes + 1, pix, chans), BF16),
                pltpu.VMEM((npairs, pix, chans), F32),
                pltpu.VMEM((npairs + 2, pix, chans), BF16),
                pltpu.VMEM((3 * chans, npairs * pix), BF16),
                pltpu.VMEM((chans, npairs * pix), BF16),
                pltpu.VMEM((12 * chans, chans), F32),
                pltpu.VMEM((3, pix, chans), F32),
                pltpu.VMEM((PIPES, BLOCK, half), BF16),
                pltpu.VMEM((PIPES, BLOCK, half), BF16),
                pltpu.VMEM((PIPES, BLOCK, half), BF16),
                pltpu.VMEM((PIPES, n * n - 1, size, half), BF16),
                pltpu.VMEM((PIPES, size, half), F32),
                pltpu.VMEM((PIPES, nz, size, half), BF16),
                pltpu.VMEM((PIPES, BLOCK, half), BF16),
                pltpu.VMEM((PIPES, BLOCK, half), BF16),
                pltpu.SemaphoreType.DMA((4,)),
                pltpu.SemaphoreType.DMA((6,)),
                pltpu.SemaphoreType.DMA((6,)),
                pltpu.SemaphoreType.DMA((PIPES, slots)),
                pltpu.SemaphoreType.DMA((PIPES, slots)),
                pltpu.SemaphoreType.REGULAR((3,)),
            ],
            compiler_params=pltpu.CompilerParams(
                collective_id=0, has_side_effects=True, vmem_limit_bytes=58 * 1024 * 1024),
            cost_estimate=pl.CostEstimate(
                flops=28 * 2 * npairs * pix * chans * chans, bytes_accessed=10 * 2**20, transcendentals=0),
            name="block",
        )(inputs, temporal_weight, spatial, pooled_grad)
        input_grad, temporal_grad, spatial_grad = pl.pallas_call(
            write_out,
            out_shape=[
                jax.ShapeDtypeStruct(inputs.shape, BF16),
                jax.ShapeDtypeStruct((3, chans, chans), F32),
                jax.ShapeDtypeStruct((9, chans, chans), F32),
            ],
            in_specs=[pl.BlockSpec(memory_space=pl.ANY)] * 3,
            out_specs=[any_spec] * 3,
            scratch_shapes=[pltpu.SemaphoreType.DMA((nframes + 12,))],
            compiler_params=pltpu.CompilerParams(vmem_limit_bytes=2**20),
            name="write_out",
        )(input_grad, temporal_grad.reshape(3, chans, chans), spatial_grad.reshape(9, chans, chans))
        return input_grad, temporal_grad, spatial_grad.reshape(3, 3, chans, chans)

    in_specs = (P("frame", "row", None, None), P(), P(), P("frame", "row", None, None))
    out_specs = (P("frame", "row", None, None), P(), P())
    return jax.shard_map(body, mesh=mesh, in_specs=in_specs, out_specs=out_specs, check_vma=False)
```

profile of v0, /device:TPU:1, one launch (start us, length us, event | category | flops | bytes accessed | tf_op | source)
XLA Modules:
  0.0 51.9 jit_solution(17514455199385375540)
XLA Ops:
  0.6 48.6 %block.1 = (bf16[8,4,128,256]{3,2,1,0:T(8,128)(2,1)S(1)}, f32[768,256]{1,0:T(8,128)S(1)}, f32[2304,256]{1,0:T(8,128)S(1)}) custom-call(bf16[8,4,128,256]{3,2,1,0:T(8,128)(2,1)} %x_hbm.1, bf16[3,256,256]{2,1,0:T(8,128)(2,1)} %tw_hbm.1, bf16[3,768,256]{2,1,0:T(8,128)(2,1)} %bitcast.7, bf16[4,4,128,256]{3,2,1,0:T(8,128)(2,1)} %g_hbm.1), custom_call_target="tpu_custom_call" | custom-call | flops 7516192768 | bytes 10485760 | tf_op jit(solution)/shard_map/block/pallas_call | solution.py:393
  49.3 2.5 %write_out.1 = (bf16[8,4,128,256]{3,2,1,0:T(8,128)(2,1)}, f32[3,256,256]{2,1,0:T(8,128)}, f32[9,256,256]{2,1,0:T(8,128)}) custom-call(bf16[8,4,128,256]{3,2,1,0:T(8,128)(2,1)S(1)} %get-tuple-element.9.grad, f32[3,256,256]{2,1,0:T(8,128)S(1)} %bitcast.5, f32[9,256,256]{2,1,0:T(8,128)S(1)} %bitcast.4), custom_call_target="tpu_custom_call" | custom-call | tf_op jit(solution)/shard_map/write_out/pallas_call | solution.py:435
where the time goes:
time: 52 us; the launch traced here: 51.9 us
  Pallas kernels  51.1 us (98%)
  between operations  0.8 us (2%)
    pallas_call x1, Pallas kernels, body(): pl.pallas_call(functools.partial(kernel, nz, n, scale), out_shape=[pltpu....  48.6 us
    pallas_call x1, Pallas kernels, body(): pl.pallas_call(write_out, out_shape=[jax.ShapeDtypeStruct(inputs.shape, B...  2.49 us

commit v1 on v0

--- a/solution.py
+++ b/solution.py
@@ -125,12 +125,14 @@
         gacc[i, pl.ds(0, edge)] += shifted(dot_t(g_rows(i, 2, nrows - 1), sw[0]))
         gacc[i, pl.ds(ncols, edge)] += shifted(dot_t(g_rows(i, 1, nrows - 1), sw[2]))
 
-    def grad_halo():
-        first = shifted(dot_t(gp[:, 0].reshape(npairs * ncols, chans), sw[2]))
-        final = shifted(dot_t(gp[:, nrows + 1].reshape(npairs * ncols, chans), sw[0]))
-        for i in range(npairs):
-            gacc[i, pl.ds(0, ncols)] += first[i * ncols:(i + 1) * ncols]
-            gacc[i, pl.ds(edge, ncols)] += final[i * ncols:(i + 1) * ncols]
+    def grad_halo(i):
+        gacc[i, pl.ds(0, ncols)] += shifted(dot_t(gp[i, 0], sw[2]))
+        gacc[i, pl.ds(edge, ncols)] += shifted(dot_t(gp[i, nrows + 1], sw[0]))
+
+    def grad_full(i):
+        wide = dot_t(g_rows(i, 2, nrows), sw[0]) + dot_t(g_rows(i, 1, nrows), sw[1])
+        gacc[i] = shifted(wide + dot_t(g_rows(i, 0, nrows), sw[2]))
+        grad_done(i)
 
     def grad_done(i):
         grad = 0.5 * gacc[i]
@@ -147,13 +149,15 @@
             total = total + outer_sum(i, left, first, count)
         taps[pl.ds(a * BLOCK, BLOCK)] = total
 
+    def spatial_edge(a):
+        left, first = (nrows - 1, nrows + 1) if a == 0 else (0, 0)
+        total = taps[pl.ds(a * BLOCK, BLOCK)]
+        for i in range(1, npairs - 1):
+            total = total + outer_sum(i, left, first, 1)
+        taps[pl.ds(a * BLOCK, BLOCK)] = total
+
     def spatial_rest(a):
         total = taps[pl.ds(a * BLOCK, BLOCK)]
-        for i in range(1, npairs - 1):
-            if a == 0:
-                total = total + outer_sum(i, nrows - 1, nrows + 1, 1)
-            if a == 2:
-                total = total + outer_sum(i, 0, 0, 1)
         for i in (0, npairs - 1):
             total = total + outer_sum(i, 0, 2 - a, nrows)
         taps[pl.ds(a * BLOCK, BLOCK)] = total
@@ -275,8 +279,7 @@
     grad_own(0)
     hear(1)
     pass_on(2)
-    for i in range(1, npairs):
-        grad_own(i)
+    grad_own(npairs - 1)
     for a in range(3):
         spatial_own(a)
     hear(2)
@@ -292,13 +295,15 @@
     def _():
         gp[:, nrows + 1] = jnp.zeros((npairs, ncols, chans), BF16)
 
-    grad_halo()
-    grad_done(0)
-    grad_done(npairs - 1)
+    for i in (0, npairs - 1):
+        grad_halo(i)
+        grad_done(i)
     grad_prev = halo(gext.at[1], gext.at[npairs + 1], 4, prv)
     grad_next = halo(gext.at[npairs], gext.at[0], 5, nxt)
     grad_prev.start()
     grad_next.start()
+    spatial_edge(0)
+    spatial_edge(2)
     x_next.wait()
     x_prev.wait()
 
@@ -318,13 +323,13 @@
     begin(0)
     spatial_rest(1)
     begin(1)
-    step_core(0)
     spatial_rest(2)
     begin(2)
+    step_core(0)
     step_core(1)
+    step_core(2)
     for i in range(1, npairs - 1):
-        grad_done(i)
-    step_core(2)
+        grad_full(i)
     temporal()
     begin(3)
     input_grad(0)

time: 52 us -> 52.4 us (level)
  no operation moved by 1% of the time
where the time goes in v1:
time: 52.4 us
  Pallas kernels  51.6 us (98%)
  between operations  0.8 us (2%)
    pallas_call x1, Pallas kernels, body(): pl.pallas_call(functools.partial(kernel, nz, n, scale), out_shape=[pltpu....  49.1 us
    pallas_call x1, Pallas kernels, body(): pl.pallas_call(write_out, out_shape=[jax.ShapeDtypeStruct(inputs.shape, B...  2.49 us

profile of v1, /device:TPU:1, one launch (start us, length us, event | category | flops | bytes accessed | tf_op | source)
XLA Modules:
  0.0 52.4 jit_solution(7322645458409096832)
XLA Ops:
  0.6 49.1 %block.1 = (bf16[8,4,128,256]{3,2,1,0:T(8,128)(2,1)S(1)}, f32[768,256]{1,0:T(8,128)S(1)}, f32[2304,256]{1,0:T(8,128)S(1)}) custom-call(bf16[8,4,128,256]{3,2,1,0:T(8,128)(2,1)} %x_hbm.1, bf16[3,256,256]{2,1,0:T(8,128)(2,1)} %tw_hbm.1, bf16[3,768,256]{2,1,0:T(8,128)(2,1)} %bitcast.7, bf16[4,4,128,256]{3,2,1,0:T(8,128)(2,1)} %g_hbm.1), custom_call_target="tpu_custom_call" | custom-call | flops 7516192768 | bytes 10485760 | tf_op jit(solution)/shard_map/block/pallas_call | solution.py:398
  49.7 2.5 %write_out.1 = (bf16[8,4,128,256]{3,2,1,0:T(8,128)(2,1)}, f32[3,256,256]{2,1,0:T(8,128)}, f32[9,256,256]{2,1,0:T(8,128)}) custom-call(bf16[8,4,128,256]{3,2,1,0:T(8,128)(2,1)S(1)} %get-tuple-element.9.grad, f32[3,256,256]{2,1,0:T(8,128)S(1)} %bitcast.5, f32[9,256,256]{2,1,0:T(8,128)S(1)} %bitcast.4), custom_call_target="tpu_custom_call" | custom-call | tf_op jit(solution)/shard_map/write_out/pallas_call | solution.py:440

commit v2 on v1

--- a/solution.py
+++ b/solution.py
@@ -63,8 +63,8 @@
     around = [peer_xy(1), peer_xy(n - 1), peer_xy(n), peer_xy(n * (n - 1)), nxt, prv]
     for device in [mate, outer] + around:
         pl.semaphore_signal(barrier, inc=1, device_id=device, device_id_type=MESH)
-    for load in loads:
-        load.start()
+    for k in (3, 2, 0, 1):
+        loads[k].start()
     pl.semaphore_wait(barrier, 2 + len(around))
 
     def pass_on(k):
@@ -323,13 +323,13 @@
     begin(0)
     spatial_rest(1)
     begin(1)
+    step_core(0)
     spatial_rest(2)
     begin(2)
-    step_core(0)
     step_core(1)
-    step_core(2)
     for i in range(1, npairs - 1):
         grad_full(i)
+    step_core(2)
     temporal()
     begin(3)
     input_grad(0)

time: 52.4 us -> 51.9 us (level)
  Pallas kernels: 51.6 us -> 51 us
    pallas_call x1, Pallas kernels: 49.1 us -> 48.5 us  [body(): pl.pallas_call(functools.partial(kernel, nz, n, scale), out_shape=[pltpu....]
where the time goes in v2:
time: 51.9 us; the launch traced here: 51.8 us
  Pallas kernels  51 us (98%)
  between operations  0.8 us (2%)
    pallas_call x1, Pallas kernels, body(): pl.pallas_call(functools.partial(kernel, nz, n, scale), out_shape=[pltpu....  48.5 us
    pallas_call x1, Pallas kernels, body(): pl.pallas_call(write_out, out_shape=[jax.ShapeDtypeStruct(inputs.shape, B...  2.49 us

profile of v2, /device:TPU:1, one launch (start us, length us, event | category | flops | bytes accessed | tf_op | source)
XLA Modules:
  0.0 51.8 jit_solution(14290336764346356107)
XLA Ops:
  0.6 48.5 %block.1 = (bf16[8,4,128,256]{3,2,1,0:T(8,128)(2,1)S(1)}, f32[768,256]{1,0:T(8,128)S(1)}, f32[2304,256]{1,0:T(8,128)S(1)}) custom-call(bf16[8,4,128,256]{3,2,1,0:T(8,128)(2,1)} %x_hbm.1, bf16[3,256,256]{2,1,0:T(8,128)(2,1)} %tw_hbm.1, bf16[3,768,256]{2,1,0:T(8,128)(2,1)} %bitcast.7, bf16[4,4,128,256]{3,2,1,0:T(8,128)(2,1)} %g_hbm.1), custom_call_target="tpu_custom_call" | custom-call | flops 7516192768 | bytes 10485760 | tf_op jit(solution)/shard_map/block/pallas_call | solution.py:398
  49.1 2.5 %write_out.1 = (bf16[8,4,128,256]{3,2,1,0:T(8,128)(2,1)}, f32[3,256,256]{2,1,0:T(8,128)}, f32[9,256,256]{2,1,0:T(8,128)}) custom-call(bf16[8,4,128,256]{3,2,1,0:T(8,128)(2,1)S(1)} %get-tuple-element.9.grad, f32[3,256,256]{2,1,0:T(8,128)S(1)} %bitcast.5, f32[9,256,256]{2,1,0:T(8,128)S(1)} %bitcast.4), custom_call_target="tpu_custom_call" | custom-call | tf_op jit(solution)/shard_map/write_out/pallas_call | solution.py:440
